TPU v7x, 128 devices: a whole 4x4x4 slice. The times are simulated.
128 devices in a mesh: wide: 32 (over z, y, core), narrow: 4 (over x).
Axes of the slice: x: 4, y: 4, z: 4, core: 2. Of those that a mesh axis runs over, the one named last changes fastest.
Arguments:
- embeddings: float32 [16384, 1024], P(('wide', 'narrow')), may hold values from -6 to 6
- cluster: int32 [16384], P(('wide', 'narrow')), may hold values from 0 to 63, as said below
- order: int32 [16384], P(('wide', 'narrow')), may hold values from 0 to 511
Outputs:
- best_similarity: float32 [16384], P(('wide', 'narrow'))
Inputs may be any that keep to these rules, and one draw needn't show every extreme that they name: Documents of one cluster have distinct order values. For every k, at most 8 documents of one device lie in clusters k * 2 to k * 2 + 1, and on every device exactly 8 for some k.
All inputs are finite; a program needn't handle non-finite values.
Results may differ from a plain program's by a relative error of at most 0.0013.
Values may be sent and summed in bfloat16 or wider, within the bound.
No kernel may reach another device: no remote copies, remote signals or barrier semaphores. Data moves between devices by JAX's collectives and lax.ppermute only.
A program may use at most 64 MiB of HBM per device.

v0:
```python
import jax
import jax.numpy as jnp
from jax import lax
from jax.sharding import PartitionSpec as P

CL_DEV = 2


epsilon = 1e-06


def per_device(embeddings, cluster, order):
    doc_dev, feature_count = embeddings.shape
    wide_count = lax.axis_size("wide")
    narrow_count = lax.axis_size("narrow")
    send_cap = 2 * doc_dev // wide_count
    capacity = narrow_count * doc_dev
    row_count = capacity // narrow_count
    slot_total = CL_DEV * capacity
    squares = jnp.sum(embeddings * embeddings, axis=1, keepdims=True)
    unit_rows = (embeddings * lax.rsqrt(squares + epsilon)).astype(jnp.bfloat16)
    owner_of = cluster // CL_DEV
    slot_index = cluster % CL_DEV * capacity + order
    one_hot = (owner_of[:, None] == jnp.arange(wide_count, dtype=jnp.int32)[None, :]).astype(
        jnp.int32
    )
    earlier = jnp.cumsum(one_hot, axis=0) - one_hot
    position = jnp.sum(earlier * one_hot, axis=1)
    target = owner_of * send_cap + position
    send_rows = (
        jnp.zeros((wide_count * send_cap, feature_count), jnp.bfloat16).at[target].set(unit_rows)
    )
    send_slots = jnp.full((wide_count * send_cap,), -1, jnp.int32).at[target].set(slot_index)
    helper = lax.axis_index("narrow")
    many_rows = jnp.broadcast_to(
        send_rows.reshape(wide_count, 1, send_cap, feature_count),
        (wide_count, narrow_count, send_cap, feature_count),
    )
    many_rows = many_rows.reshape(wide_count * narrow_count * send_cap, feature_count)
    many_slots = jnp.broadcast_to(
        send_slots.reshape(wide_count, 1, send_cap), (wide_count, narrow_count, send_cap)
    ).reshape(-1)
    got_rows, got_slots = (
        lax.all_to_all(many_rows, ("wide", "narrow"), split_axis=0, concat_axis=0, tiled=True),
        lax.all_to_all(many_slots, ("wide", "narrow"), split_axis=0, concat_axis=0, tiled=True),
    )
    slot_table = jnp.zeros((slot_total, feature_count), jnp.bfloat16)
    slot_live = jnp.zeros((slot_total,), jnp.float32)
    drop_index = jnp.where(got_slots >= 0, got_slots, slot_total)
    slot_table, slot_live = (
        slot_table.at[drop_index].set(got_rows, mode="drop"),
        slot_live.at[drop_index].set(1.0, mode="drop"),
    )
    back_slots = lax.dynamic_index_in_dim(
        got_slots.reshape(wide_count, narrow_count, send_cap), helper, axis=1, keepdims=False
    )
    slot_table = slot_table.reshape(CL_DEV, capacity, feature_count)
    slot_live = slot_live.reshape(CL_DEV, capacity)
    row_start = helper * row_count
    all_positions = jnp.arange(capacity, dtype=jnp.int32)
    own_positions = row_start + jnp.arange(row_count, dtype=jnp.int32)

    def by_rows(operands):
        key_rows, key_live = operands
        queries = lax.dynamic_slice_in_dim(key_rows, row_start, row_count, 0)
        similar = jnp.einsum("qe,ke->qk", queries, key_rows, preferred_element_type=jnp.float32)
        allowed = (all_positions[None, :] < own_positions[:, None]) & (key_live[None, :] > 0)
        return jnp.max(jnp.where(allowed, similar, jnp.float32(-1.0)), axis=1)

    partial_value = lax.map(by_rows, (slot_table, slot_live))
    best_value = lax.all_gather(partial_value, "narrow", axis=1, tiled=True)
    flat_best = best_value.reshape(-1)
    values = jnp.where(
        back_slots >= 0, flat_best[jnp.clip(back_slots, 0, slot_total - 1)], jnp.float32(0.0)
    )
    returned = lax.all_to_all(values, "wide", split_axis=0, concat_axis=0, tiled=True)
    return returned.reshape(-1)[target]


def solution(mesh):
    in_specs = (P(("wide", "narrow"), None), P(("wide", "narrow")), P(("wide", "narrow")))
    out_specs = P(("wide", "narrow"))
    return jax.shard_map(
        per_device, mesh=mesh, in_specs=in_specs, out_specs=out_specs, check_vma=False
    )
```

profile of v0, /device:TPU:0, one launch (start us, length us, event | category | flops | bytes accessed | tf_op | source)
XLA Modules:
  0.0 95.4 jit_solution(3273551868931262391)
XLA Ops:
  0.0 0.7 fusion.21
  0.7 0.1 fusion.17
  0.8 0.2 reduce_window_sum.11
  0.9 0.2 select_reduce_fusion
  1.1 1.0 %scatter_custom_fusion = s32[256]{0:T(256)S(1)} fusion(s32[128]{0:T(128)S(1)} %compare_select_fusion.4, s32[128]{0:T(128)S(1)} %get-tuple-element.159, s32[]{:T(128)} %constant.132.clone.1), kind=kCustom, calls=%fused_computation.48 | custom fusion | bytes 1028 | tf_op jit(solution)/shard_map/scatter | solution.py:33
  2.1 0.1 broadcast_in_dim.72
  2.2 0.6 broadcast_in_dim.73
  2.8 11.1 %all-to-all-start = ((s32[128,8,1]{1,2,0:T(1,128)}), s32[128,8,1]{1,2,0:T(1,128)S(1)}, u32[]{:S(2)}, u32[]{:S(2)}) async-start(s32[128,8,1]{1,2,0:T(1,128)} %bitcast), calls=%async_computation | async-start | bytes 131072 | tf_op jit(solution)/shard_map/all_to_all | solution.py:45
  14.0 1.2 %multiply_reduce_fusion = f32[128]{0:T(128)S(1)} fusion(f32[128,1024]{1,0:T(8,128)} %param.5), kind=kLoop, calls=%fused_computation.23 | loop fusion | flops 262016 | bytes 524800 | tf_op jit(solution)/shard_map/reduce_sum | solution.py:20
  15.2 1.9 %scatter_custom_fusion.2 = bf16[256,1024]{1,0:T(8,128)(2,1)S(1)} fusion(s32[128]{0:T(128)S(1)} %compare_select_fusion.4, f32[128,1024]{1,0:T(8,128)} %param.5, f32[128]{0:T(128)S(1)} %add_rsqrt_fusion, bf16[]{:T(256)} %constant.142.clone.1), kind=kCustom, calls=%fused_computation.24 | custom fusion | flops 262144 | bytes 1049090 | tf_op jit(solution)/shard_map/scatter | solution.py:31
  17.1 6.2 %all-to-all-done = s32[128,8,1]{1,2,0:T(1,128)S(1)} async-done(((s32[128,8,1]{1,2,0:T(1,128)}), s32[128,8,1]{1,2,0:T(1,128)S(1)}, u32[]{:S(2)}, u32[]{:S(2)}) %all-to-all-start) | async-done | bytes 4128 | tf_op jit(solution)/shard_map/all_to_all | solution.py:45
  23.3 1.6 %broadcast_in_dim.81 = bf16[32,4,8,1024]{3,2,1,0:T(8,128)(2,1)} broadcast(bf16[32,8,1024]{2,1,0:T(8,128)(2,1)S(1)} %bitcast.30), dimensions={0,2,3} | broadcast | bytes 2621440 | tf_op jit(solution)/shard_map/broadcast_in_dim | solution.py:35
  24.9 4.7 %all-to-all-start.1 = ((bf16[128,8,1024]{2,1,0:T(8,128)(2,1)}), bf16[128,8,1024]{2,1,0:T(8,128)(2,1)S(1)}, u32[]{:S(2)}, u32[]{:S(2)}) async-start(bf16[128,8,1024]{2,1,0:T(8,128)(2,1)} %bitcast.4), calls=%async_computation.1 | async-start | bytes 4194304 | tf_op jit(solution)/shard_map/all_to_all | solution.py:44
  29.6 0.5 broadcast.147
  30.1 0.8 reduce.8
  30.9 0.1 all_to_all.22
  31.0 4.3 %scatter_custom_fusion.1 = f32[1024]{0:T(1024)S(1)} fusion(s32[1024]{0:T(1024)S(1)} %bitcast.38, f32[1024]{0:T(1024)S(1)} %broadcast.110, f32[]{:T(128)} %constant.141.clone.1), kind=kCustom, calls=%fused_computation.38 | custom fusion | bytes 4100 | tf_op jit(solution)/shard_map/scatter | solution.py:52
  35.4 0.1 reshape.103
  35.5 24.2 %all-to-all-done.1 = bf16[128,8,1024]{2,1,0:T(8,128)(2,1)S(1)} async-done(((bf16[128,8,1024]{2,1,0:T(8,128)(2,1)}), bf16[128,8,1024]{2,1,0:T(8,128)(2,1)S(1)}, u32[]{:S(2)}, u32[]{:S(2)}) %all-to-all-start.1) | async-done | bytes 2097184 | tf_op jit(solution)/shard_map/all_to_all | solution.py:44
  59.7 6.8 %scatter_custom_fusion.3 = bf16[1024,1024]{1,0:T(8,128)(2,1)} fusion(s32[1024]{0:T(1024)S(1)} %bitcast.39, bf16[128,8,1024]{2,1,0:T(8,128)(2,1)S(1)} %all-to-all-done.1, bf16[]{:T(256)} %constant.142.clone.1), kind=kCustom, calls=%fused_computation.19 | custom fusion | bytes 4194306 | tf_op jit(solution)/shard_map/scatter | solution.py:51
  66.6 4.0 %while.14 = (s32[]{:T(128)}, f32[2,128]{1,0:T(2,128)S(1)}, f32[2,512]{1,0:T(2,128)S(1)}, bf16[2,512,1024]{2,1,0:T(8,128)(2,1)}, s32[]{:T(128)}, /*index=5*/s32[]{:T(128)}, s32[]{:T(128)}, s32[]{:T(128)}) while((s32[]{:T(128)}, f32[2,128]{1,0:T(2,128)S(1)}, f32[2,512]{1,0:T(2,128)S(1)}, bf16[2,512,1024]{2,1,0:T(8,128)(2,1)}, ...), condition=%wide.region_9.10_spmd.clone, body=%wide.region_7.9_spmd.clone.sunk | while | flops 134480384 | bytes 1317493 | solution.py:70
  66.6 1.9 %fusion.29 = f32[128]{0:T(128)S(1)} fusion(bf16[2,512,1024]{2,1,0:T(8,128)(2,1)} %get-tuple-element.217, s32[]{:T(128)} %get-tuple-element.206, s32[]{:T(128)S(6)} %dynamic_slice.51, s32[]{:T(128)} %get-tuple-element.218, s32[128]{0:T(128)S(1)} %iota_add_fusion.2, pred[512]{0:T(512)(128)(4,1)S(1)} %compare_reduce_fusion.2), kind=kOutput, calls=%fused_computation.9.clone.1 | convolution fusion | flops 134479744 | bytes 1313284 | tf_op jit(solution)/shard_map/while/body/eval_jaxpr/qe,ke->qk/dot_general | solution.py:66
  68.6 1.9 %fusion.29 = f32[128]{0:T(128)S(1)} fusion(bf16[2,512,1024]{2,1,0:T(8,128)(2,1)} %get-tuple-element.217, s32[]{:T(128)} %get-tuple-element.206, s32[]{:T(128)S(6)} %dynamic_slice.51, s32[]{:T(128)} %get-tuple-element.218, s32[128]{0:T(128)S(1)} %iota_add_fusion.2, pred[512]{0:T(512)(128)(4,1)S(1)} %compare_reduce_fusion.2), kind=kOutput, calls=%fused_computation.9.clone.1 | convolution fusion | flops 134479744 | bytes 1313284 | tf_op jit(solution)/shard_map/while/body/eval_jaxpr/qe,ke->qk/dot_general | solution.py:66
  70.5 8.5 %all_gather.3 = f32[2,512]{1,0:T(2,128)S(1)} all-gather(f32[2,128]{1,0:T(2,128)S(1)} %get-tuple-element.130), channel_id=1, replica_groups=mesh['wide'=32,'narrow'=4] {'narrow'}, dimensions={1}, use_global_device_ids=true | all-gather | bytes 5120 | tf_op jit(solution)/shard_map/all_gather | solution.py:71
  79.0 1.4 %gather_fusion = f32[256]{0:T(256)S(1)} fusion(f32[1024]{0:T(1024)S(1)} %bitcast.29, s32[1024]{0:T(1024)S(1)} %pad_clamp_fusion.1), kind=kCustom, calls=%fused_computation | custom fusion | bytes 3072 | tf_op jit(solution)/shard_map/gather | solution.py:74
  80.5 0.6 compare_select_fusion
  81.1 3.9 %all-to-all-start.2 = ((f32[32,1,8]{2,1,0:T(1,128)}), f32[32,1,8]{2,1,0:T(1,128)S(1)}, u32[]{:S(2)}, u32[]{:S(2)}) async-start(f32[32,1,8]{2,1,0:T(1,128)} %compare_select_fusion), calls=%async_computation.2 | async-start | bytes 32768 | tf_op jit(solution)/shard_map/all_to_all | solution.py:76
  85.0 7.3 %all-to-all-done.2 = f32[32,1,8]{2,1,0:T(1,128)S(1)} async-done(((f32[32,1,8]{2,1,0:T(1,128)}), f32[32,1,8]{2,1,0:T(1,128)S(1)}, u32[]{:S(2)}, u32[]{:S(2)}) %all-to-all-start.2) | async-done | bytes 1056 | tf_op jit(solution)/shard_map/all_to_all | solution.py:76
  92.3 0.5 broadcast.148
  92.8 0.7 reduce.9
  93.5 0.1 reshape.100
  93.6 1.8 %gather_fusion.1 = f32[128]{0:T(128)} fusion(f32[256]{0:T(256)S(1)} %reshape.100, s32[1024]{0:T(1024)S(1)} %pad_clamp_fusion), kind=kCustom, calls=%fused_computation.1 | custom fusion | bytes 1536 | tf_op jit(solution)/shard_map/gather | solution.py:77
  (18 shorter events, 0.3 us)
Async XLA Ops:
  2.8 20.4 %all-to-all-start = ((s32[128,8,1]{1,2,0:T(1,128)}), s32[128,8,1]{1,2,0:T(1,128)S(1)}, u32[]{:S(2)}, u32[]{:S(2)}) async-start(s32[128,8,1]{1,2,0:T(1,128)} %bitcast), calls=%async_computation | async-start | bytes 131072 | tf_op jit(solution)/shard_map/all_to_all | solution.py:45
  24.9 34.8 %all-to-all-start.1 = ((bf16[128,8,1024]{2,1,0:T(8,128)(2,1)}), bf16[128,8,1024]{2,1,0:T(8,128)(2,1)S(1)}, u32[]{:S(2)}, u32[]{:S(2)}) async-start(bf16[128,8,1024]{2,1,0:T(8,128)(2,1)} %bitcast.4), calls=%async_computation.1 | async-start | bytes 4194304 | tf_op jit(solution)/shard_map/all_to_all | solution.py:44
  81.1 11.2 %all-to-all-start.2 = ((f32[32,1,8]{2,1,0:T(1,128)}), f32[32,1,8]{2,1,0:T(1,128)S(1)}, u32[]{:S(2)}, u32[]{:S(2)}) async-start(f32[32,1,8]{2,1,0:T(1,128)} %compare_select_fusion), calls=%async_computation.2 | async-start | bytes 32768 | tf_op jit(solution)/shard_map/all_to_all | solution.py:76
where the time goes:
time: 96.6 us; the launch traced here: 95.4 us
  waiting for transfers between devices  37.8 us (39%)
  starting transfers between devices  19.6 us (20%)
  local copies, waits for them, and re-layouts  19.1 us (20%)
  blocking collectives  8.48 us (9%)
  other arithmetic  6.39 us (7%)
  matrix products  3.8 us (4%)
    all_to_all x1, waiting for transfers between devices, per_device(): lax.all_to_all(many_rows, ('wide', 'narrow'), split_axis=0, concat_axis=0...  24.2 us
    all_to_all x1, starting transfers between devices, per_device(): lax.all_to_all(many_slots, ('wide', 'narrow'), split_axis=0, concat_axis=...  11.1 us
    all_gather x1, blocking collectives, per_device(): best_value = lax.all_gather(partial_value, 'narrow', axis=1, tiled=True)  8.48 us
    all_to_all x1, waiting for transfers between devices, per_device(): lax.all_to_all(values, 'wide', split_axis=0, concat_axis=0, tiled=True)  7.33 us
    scatter x1, local copies, waits for them, and re-layouts, per_device(): slot_table.at[drop_index].set(got_rows, mode='drop')  6.84 us
    all_to_all x1, waiting for transfers between devices, per_device(): lax.all_to_all(many_slots, ('wide', 'narrow'), split_axis=0, concat_axis=...  6.24 us
    all_to_all x1, starting transfers between devices, per_device(): lax.all_to_all(many_rows, ('wide', 'narrow'), split_axis=0, concat_axis=0...  4.65 us
    scatter x1, local copies, waits for them, and re-layouts, per_device(): slot_live.at[drop_index].set(1.0, mode='drop')  4.31 us
  transfers between devices with their start and end apart: 3, of which 3 were waited for; matrix products, arithmetic and copies ran while one was open for 9% of the time, Pallas kernels for 0%

commit v1 on v0

v1 whole, which is shorter than its diff:
```python
import jax
import jax.numpy as jnp
from jax import lax
from jax.experimental import pallas as pl
from jax.experimental.pallas import tpu as pltpu
from jax.sharding import Mesh, PartitionSpec as P

CLUSTERS = 64
SLOTS = 8
CAP = 512
LANES = 128
CORES = 2
epsilon = 1e-06

VMEM = 32 * 1024 * 1024
NT = (((1,), (1,)), ((), ()))
TN = (((0,), (0,)), ((), ()))


def iota(shape, axis):
    return lax.broadcasted_iota(jnp.int32, shape, axis)


def as_bf16(mask):
    return jnp.where(mask, 1.0, 0.0).astype(jnp.bfloat16)


def pack_kernel(rows_ref, cluster_ref, order_ref, out_ref, position_ref):
    docs, width = rows_ref.shape
    slots = out_ref.shape[0]
    cluster = cluster_ref[...]
    member = iota((CLUSTERS, docs), 0) == cluster
    before = as_bf16(iota((docs, docs), 0) < iota((docs, docs), 1))
    count = jnp.dot(as_bf16(member), before, preferred_element_type=jnp.float32)
    position = jnp.sum(jnp.where(member, count, 0.0), axis=0, keepdims=True).astype(jnp.int32)
    position_ref[...] = position
    target = cluster * SLOTS + position
    place = as_bf16(iota((slots, docs), 0) == target)
    rank = order_ref[...] - CAP
    high = (rank >> 4).astype(jnp.float32)
    low = (rank & 15).astype(jnp.float32)
    line = iota((LANES, docs), 0)
    ranks = jnp.where(line == 0, high, jnp.where(line == 1, low, 0.0)).astype(jnp.bfloat16)
    out_ref[:, width:] = lax.dot_general(
        place, ranks, NT, preferred_element_type=jnp.float32
    ).astype(jnp.bfloat16)
    rows = rows_ref[...]
    squares = jnp.sum(rows * rows, axis=1, keepdims=True)
    unit = (rows * lax.rsqrt(squares + epsilon)).astype(jnp.bfloat16)
    out_ref[:, :width] = jnp.dot(place, unit, preferred_element_type=jnp.float32).astype(
        jnp.bfloat16
    )


def best_of(query_ref, key_ref, width, first):
    keys = key_ref.shape[0]
    weight_lane = iota((8, LANES), 1)
    weight = jnp.where(weight_lane == 0, 16.0, jnp.where(weight_lane == 1, 1.0, 0.0)).astype(
        jnp.bfloat16
    )
    key_rank = lax.dot_general(
        weight, key_ref[:, width:], NT, preferred_element_type=jnp.float32
    )[0:1]
    spread_line = iota((LANES, LANES), 0)
    spread = jnp.where(spread_line == 0, 16.0, jnp.where(spread_line == 1, 1.0, 0.0)).astype(
        jnp.bfloat16
    )
    query_rank = jnp.dot(query_ref[:, width:], spread, preferred_element_type=jnp.float32)
    similar = lax.dot_general(
        query_ref[:, :width], key_ref[:, :width], NT, preferred_element_type=jnp.float32
    )
    best = first
    for at in range(0, keys, LANES):
        allowed = key_rank[:, at : at + LANES] < query_rank
        best = jnp.maximum(best, jnp.where(allowed, similar[:, at : at + LANES], -1.0))
    return best


def own_kernel(own_ref, best_ref):
    width = own_ref.shape[1] - LANES
    best_ref[...] = best_of(own_ref, own_ref, width, jnp.float32(-1.0))


def other_kernel(own_ref, other_ref, first_ref, out_ref):
    width = own_ref.shape[1] - LANES
    best = best_of(own_ref, other_ref, width, first_ref[...])
    best = jnp.max(best, axis=1, keepdims=True)
    slots = own_ref.shape[0]
    mine = iota((slots, LANES), 1) == iota((slots, LANES), 0) % SLOTS
    spread = jnp.where(mine, best, 0.0).reshape(slots // SLOTS, SLOTS, LANES)
    out_ref[...] = jnp.sum(spread, axis=1)


def unpack_kernel(best_ref, cluster_ref, position_ref, out_ref):
    docs = cluster_ref.shape[1]
    member = jnp.where(iota((CLUSTERS, docs), 0) == cluster_ref[...], 1.0, 0.0)
    by_slot = lax.dot_general(
        best_ref[...],
        member,
        TN,
        precision=lax.Precision.HIGHEST,
        preferred_element_type=jnp.float32,
    )
    wanted = iota((LANES, docs), 0) == position_ref[...]
    out_ref[...] = jnp.sum(jnp.where(wanted, by_slot, 0.0), axis=0, keepdims=True)


def call(kernel, out_shape, flops, moved):
    return pl.pallas_call(
        kernel,
        out_shape=out_shape,
        compiler_params=pltpu.CompilerParams(vmem_limit_bytes=VMEM),
        cost_estimate=pl.CostEstimate(flops=flops, bytes_accessed=moved, transcendentals=0),
    )


def per_device(embeddings, cluster, order):
    docs, width = embeddings.shape
    slots = CLUSTERS * SLOTS
    wide = width + LANES
    f32 = jnp.float32
    cluster, order = cluster.reshape(1, docs), order.reshape(1, docs)
    packed, position = call(
        pack_kernel,
        (
            jax.ShapeDtypeStruct((slots, wide), jnp.bfloat16),
            jax.ShapeDtypeStruct((1, docs), jnp.int32),
        ),
        2 * slots * docs * wide,
        docs * width * 4 + slots * wide * 2,
    )(embeddings, cluster, order)
    own = lax.all_to_all(packed, ("zy", "x"), split_axis=0, concat_axis=0, tiled=True)
    other = lax.ppermute(own, "core", [(0, 1), (1, 0)])
    flops = 2 * slots * slots * width
    first = call(
        own_kernel, jax.ShapeDtypeStruct((slots, LANES), f32), flops, slots * wide * 2
    )(own)
    best = call(
        other_kernel,
        jax.ShapeDtypeStruct((CLUSTERS, LANES), f32),
        flops,
        2 * slots * wide * 2,
    )(own, other, first)
    back = lax.all_to_all(best, ("zy", "x"), split_axis=0, concat_axis=0, tiled=True)
    result = call(
        unpack_kernel, jax.ShapeDtypeStruct((1, docs), f32), 0, CLUSTERS * LANES * 4
    )(back, cluster, position)
    return result.reshape(docs)


def solution(mesh):
    devices = mesh.devices.reshape(-1, CORES, mesh.shape["narrow"])
    chips = Mesh(devices, ("zy", "core", "x"))
    axes = ("zy", "core", "x")
    return jax.shard_map(
        per_device,
        mesh=chips,
        in_specs=(P(axes, None), P(axes), P(axes)),
        out_specs=P(axes),
        check_vma=False,
    )
```

time: 96.6 us -> 53.5 us (0.55); the launches traced: 95.4 us -> 53.3 us
  blocking collectives: 8.48 us -> 45.8 us
  waiting for transfers between devices: 37.8 us -> 2.06 us
  starting transfers between devices: 19.6 us -> 0.01 us
  local copies, waits for them, and re-layouts: 19.1 us -> 2.36 us
  other arithmetic: 6.39 us -> 0 us
  matrix products: 3.8 us -> 0 us
  Pallas kernels: 0 us -> 3.03 us
    all_to_all x0 -> x2, blocking collectives: none -> 45.8 us  [the longest x1 31.6 us: per_device(): lax.all_to_all(packed, ('zy', 'x'), split_axis=0, concat_axis=0, tiled=True)]
    all_to_all x3 -> x0, waiting for transfers between devices: 37.8 us -> none  [the longest x1 24.2 us: per_device(): lax.all_to_all(many_rows, ('wide', 'narrow'), split_axis=0, concat_axis=0...]
    all_to_all x3 -> x0, starting transfers between devices: 19.6 us -> none  [the longest x1 11.1 us: per_device(): lax.all_to_all(many_slots, ('wide', 'narrow'), split_axis=0, concat_axis=...]
    scatter x3 -> x0, local copies, waits for them, and re-layouts: 12.1 us -> none  [the longest x1 6.84 us: per_device(): slot_table.at[drop_index].set(got_rows, mode='drop')]
    all_gather x1 -> x0, blocking collectives: 8.48 us -> none  [per_device(): best_value = lax.all_gather(partial_value, 'narrow', axis=1, tiled=True)]
    dot_general x2 -> x0, matrix products: 3.8 us -> none  [by_rows(): jnp.einsum('qe,ke->qk', queries, key_rows, preferred_element_type=jnp.flo...]
    gather x3 -> x0, local copies, waits for them, and re-layouts: 3.21 us -> none  [the longest x1 1.77 us: per_device(): return returned.reshape(-1)[target]]
    pallas_call x0 -> x4, Pallas kernels: none -> 3.03 us  [the longest x1 0.87 us: per_device(): call(other_kernel, jax.ShapeDtypeStruct((CLUSTERS, LANES), f32), flops, 2...]
  transfers between devices with their start and end apart: 3 -> 1, of which waited for: 3 -> 1; matrix products, arithmetic and copies ran while one was open for 9% -> 0% of each run, Pallas kernels for 0% -> 1%
where the time goes in v1:
time: 53.5 us; the launch traced here: 53.3 us
  blocking collectives  45.8 us (86%)
  Pallas kernels  3.03 us (6%)
  local copies, waits for them, and re-layouts  2.36 us (4%)
  waiting for transfers between devices  2.06 us (4%)
    all_to_all x1, blocking collectives, per_device(): lax.all_to_all(packed, ('zy', 'x'), split_axis=0, concat_axis=0, tiled=True)  31.6 us
    all_to_all x1, blocking collectives, per_device(): lax.all_to_all(best, ('zy', 'x'), split_axis=0, concat_axis=0, tiled=True)  14.2 us
    unnamed x8, local copies, waits for them, and re-layouts  2.36 us
    ppermute x1, waiting for transfers between devices, per_device(): other = lax.ppermute(own, 'core', [(0, 1), (1, 0)])  2.06 us
  transfers between devices with their start and end apart: 1, of which 1 were waited for; matrix products, arithmetic and copies ran while one was open for 0% of the time, Pallas kernels for 1%

profile of v1, /device:TPU:0, one launch (start us, length us, event | category | flops | bytes accessed | tf_op | source)
XLA Modules:
  0.0 53.3 jit_solution(9469582137842506687)
XLA Ops:
  0.0 0.0 copy-start
  0.0 0.7 %copy-done = s32[128]{0:T(128)S(1)} copy-done((s32[128]{0:T(128)S(1)}, s32[128]{0:T(128)}, u32[]{:S(2)}) %copy-start) | copy-done | bytes 536
  0.7 0.0 copy-start.2
  0.7 1.0 %copy-done.2 = f32[128,1024]{1,0:T(8,128)S(1)} copy-done((f32[128,1024]{1,0:T(8,128)S(1)}, f32[128,1024]{1,0:T(8,128)}, u32[]{:S(2)}) %copy-start.2) | copy-done | bytes 524312
  1.7 0.0 copy-start.3
  1.7 0.7 %copy-done.3 = s32[128]{0:T(128)S(1)} copy-done((s32[128]{0:T(128)S(1)}, s32[128]{0:T(128)}, u32[]{:S(2)}) %copy-start.3) | copy-done | bytes 536
  2.4 0.6 %shard_map.37 = (bf16[512,1152]{1,0:T(8,128)(2,1)S(1)}, s32[1,128]{1,0:T(1,128)S(1)}) custom-call(f32[128,1024]{1,0:T(8,128)S(1)} %copy-done.2, s32[1,128]{1,0:T(1,128)S(1)} %bitcast.15, s32[1,128]{1,0:T(1,128)S(1)} %bitcast.17), custom_call_target="tpu_custom_call" | custom-call | flops 150994944 | bytes 1703936 | tf_op jit(solution)/shard_map/pallas_call | solution.py:123
  3.0 31.6 %all_to_all.22 = bf16[64,8,1152]{2,1,0:T(8,128)(2,1)S(1)} all-to-all(bf16[64,8,1152]{2,1,0:T(8,128)(2,1)S(1)} %bitcast.12), channel_id=1, replica_groups=mesh['zy'=16,'core'=2,'x'=4] {'zy','x'}, dimensions={0} | all-to-all | bytes 2359296 | tf_op jit(solution)/shard_map/all_to_all | solution.py:132
  34.5 0.0 collective-permute-start
  34.5 0.8 %shard_map.38.first_ref = f32[512,128]{1,0:T(8,128)S(1)} custom-call(bf16[512,1152]{1,0:T(8,128)(2,1)S(1)} %bitcast.10), custom_call_target="tpu_custom_call" | custom-call | flops 536870912 | bytes 1179648 | tf_op jit(solution)/shard_map/pallas_call | solution.py:135
  35.3 0.0 copy-start.1
  35.3 2.1 %collective-permute-done.other_ref = bf16[512,1152]{1,0:T(8,128)(2,1)S(1)} collective-permute-done((bf16[512,1152]{1,0:T(8,128)(2,1)S(1)}, bf16[512,1152]{1,0:T(8,128)(2,1)S(1)}, u32[]{:S(2)}, u32[]{:S(2)}) %collective-permute-start) | collective-permute-done | bytes 1179680 | tf_op jit(solution)/shard_map/ppermute | solution.py:133
  37.4 0.9 %shard_map.39 = f32[64,128]{1,0:T(8,128)S(1)} custom-call(bf16[512,1152]{1,0:T(8,128)(2,1)S(1)} %bitcast.11, bf16[512,1152]{1,0:T(8,128)(2,1)S(1)} %collective-permute-done.other_ref, f32[512,128]{1,0:T(8,128)S(1)} %shard_map.38.first_ref), custom_call_target="tpu_custom_call" | custom-call | flops 536870912 | bytes 2359296 | tf_op jit(solution)/shard_map/pallas_call | solution.py:138
  38.3 14.2 %all_to_all.23 = f32[64,1,128]{2,1,0:T(1,128)S(1)} all-to-all(f32[64,1,128]{2,1,0:T(1,128)S(1)} %bitcast.14), channel_id=1, replica_groups=mesh['zy'=16,'core'=2,'x'=4] {'zy','x'}, dimensions={0} | all-to-all | bytes 65536 | tf_op jit(solution)/shard_map/all_to_all | solution.py:144
  52.5 0.0 copy-done.1
  52.5 0.8 %shard_map.40 = f32[1,128]{1,0:T(1,128)} custom-call(f32[64,128]{1,0:T(8,128)S(1)} %bitcast.13, s32[1,128]{1,0:T(1,128)S(1)} %bitcast.16, s32[1,128]{1,0:T(1,128)S(1)} %get-tuple-element.8.position_ref), custom_call_target="tpu_custom_call" | custom-call | bytes 32768 | tf_op jit(solution)/shard_map/pallas_call | solution.py:145
Async XLA Ops:
  0.0 0.7 %copy-start = (s32[128]{0:T(128)S(1)}, s32[128]{0:T(128)}, u32[]{:S(2)}) copy-start(s32[128]{0:T(128)} %param.4) | copy-start | bytes 1540
  0.7 1.0 %copy-start.2 = (f32[128,1024]{1,0:T(8,128)S(1)}, f32[128,1024]{1,0:T(8,128)}, u32[]{:S(2)}) copy-start(f32[128,1024]{1,0:T(8,128)} %rows_ref.1) | copy-start | bytes 1572868
  1.7 0.7 %copy-start.3 = (s32[128]{0:T(128)S(1)}, s32[128]{0:T(128)}, u32[]{:S(2)}) copy-start(s32[128]{0:T(128)} %param.5) | copy-start | bytes 1540
  34.5 2.8 %collective-permute-start = (bf16[512,1152]{1,0:T(8,128)(2,1)S(1)}, bf16[512,1152]{1,0:T(8,128)(2,1)S(1)}, u32[]{:S(2)}, u32[]{:S(2)}) collective-permute-start(bf16[512,1152]{1,0:T(8,128)(2,1)S(1)} %bitcast.9), channel_id=1, source_target_pairs={{0,4},{4,0},{1,5},{5,1},{2,6},{6,2},{3,7},{7,3},{8,12},{12,8},{9,1... | collective-permute-start | bytes 3538952 | tf_op jit(solution)/shard_map/ppermute | solution.py:133
  35.3 17.2 %copy-start.1 = (s32[128]{0:T(128)S(1)}, s32[128]{0:T(128)}, u32[]{:S(2)}) copy-start(s32[128]{0:T(128)} %param.4) | copy-start | bytes 1540
